TPU v7x, 32 devices: a whole 2x2x4 slice. The times are simulated.
32 devices in a mesh: dp: 8 (over z, y), fsdp: 4 (over x, core).
Axes of the slice: x: 2, y: 2, z: 4, core: 2. Of those that a mesh axis runs over, the one named last changes fastest.
Arguments:
- features: bfloat16 [32, 8, 256, 128], P(('dp', 'fsdp')), may hold values from -60 to 60, as said below
- pick_index: int32 [32, 8, 2], P(('dp', 'fsdp')), may hold values from 0 to 255
- good_channel: int32 [32, 8], P(('dp', 'fsdp')), may hold values 0 or 1
- conv_weight: bfloat16 [1152, 128], P(None, 'fsdp'), may hold values from -0.1875 to 0.1875
- conv_bias: bfloat16 [1, 128], P(None, 'fsdp'), may hold values from -3 to 3
- head_weight: bfloat16 [2, 128], P(None, 'fsdp'), may hold values from -0.5 to 0.5
- head_bias: float32 [2], replicated, may hold values from -2 to 2
Outputs:
- grad_conv_weight: float32 [1152, 128], P('dp', 'fsdp')
- grad_conv_bias: float32 [1, 128], P(None, 'fsdp')
- grad_head_weight: float32 [2, 128], P(None, 'fsdp')
- grad_head_bias: float32 [2], replicated
- grad_features: bfloat16 [32, 8, 256, 128], P(('dp', 'fsdp'))
Inputs may be any that keep to these rules, and one draw needn't show every extreme that they name: `features`: real-valued feature maps.
All inputs are finite; a program needn't handle non-finite values. No bound on the sum of `good_channel` on one device may be relied on, other than what follows from the above.
Results may differ from a plain program's by a relative error of at most 0.007.
Values may be sent and summed in bfloat16 or wider, within the bound.
A program may use at most 64 MiB of HBM per device.

v0:
```python
import jax
import jax.numpy as jnp
from jax import lax
from jax.sharding import PartitionSpec as P

SIGMA = 20


def local_grads(features, pick_index, good_channel, conv_weight, conv_bias, head_weight, head_bias):
    patch_count, row_count, sample_count, width = features.shape
    cells = patch_count * row_count * sample_count
    padded = jnp.pad(features, ((0, 0), (1, 1), (1, 1), (0, 0)))
    preact = jnp.zeros((cells, width), jnp.float32) + conv_bias.astype(jnp.float32)
    shifted = []
    for tap_index in range(9):
        offset_row = tap_index // 3
        offset_col = tap_index % 3
        window = padded[
            :, offset_row : offset_row + row_count, offset_col : offset_col + sample_count, :
        ].reshape(cells, width)
        shifted.append(window)
        preact = preact + jnp.dot(
            window,
            conv_weight[tap_index * width : (tap_index + 1) * width],
            preferred_element_type=jnp.float32,
        )
    gate_value = jax.nn.sigmoid(preact)
    hidden = (preact * gate_value).astype(jnp.bfloat16)
    slope_term = gate_value * (1.0 + preact * (1.0 - gate_value))
    logits = (
        jnp.einsum("kc,nc->kn", head_weight, hidden, preferred_element_type=jnp.float32)
        + head_bias[:, None]
    )
    positions = jnp.arange(sample_count, dtype=jnp.float32)
    arrival = jnp.transpose(pick_index, (2, 0, 1)).astype(jnp.float32)[..., None]
    target = jnp.exp(-((positions - arrival) ** 2) / (2.0 * SIGMA * SIGMA)).reshape(2, cells)
    usable = jnp.broadcast_to(
        good_channel.astype(jnp.float32)[:, :, None], (patch_count, row_count, sample_count)
    ).reshape(1, cells)
    dlogit = (usable * (jax.nn.sigmoid(logits) - target)).astype(jnp.bfloat16)
    grad_head_weight = jnp.dot(dlogit, hidden, preferred_element_type=jnp.float32)
    grad_head_bias = jnp.sum(dlogit.astype(jnp.float32), axis=1)
    dact = jnp.einsum("kn,kc->nc", dlogit, head_weight, preferred_element_type=jnp.float32)
    dpre = (dact * slope_term).astype(jnp.bfloat16)
    grad_conv_bias = jnp.sum(dpre.astype(jnp.float32), axis=0)[None, :]
    blocks = [
        jnp.einsum("nc,nd->cd", window, dpre, preferred_element_type=jnp.float32)
        for window in shifted
    ]
    grad_conv_weight = jnp.concatenate(blocks, axis=0)
    dpad = jnp.pad(
        dpre.reshape(patch_count, row_count, sample_count, width), ((0, 0), (1, 1), (1, 1), (0, 0))
    )
    back = jnp.zeros((cells, width), jnp.float32)
    for tap_index in range(9):
        offset_row = tap_index // 3
        offset_col = tap_index % 3
        window = dpad[
            :,
            2 - offset_row : 2 - offset_row + row_count,
            2 - offset_col : 2 - offset_col + sample_count,
            :,
        ].reshape(cells, width)
        back = back + jnp.einsum(
            "nd,cd->nc",
            window,
            conv_weight[tap_index * width : (tap_index + 1) * width],
            preferred_element_type=jnp.float32,
        )
    grad_features = back.astype(jnp.bfloat16).reshape(patch_count, row_count, sample_count, width)
    return (grad_conv_weight, grad_conv_bias, grad_head_weight, grad_head_bias, grad_features)


def on_device(features, pick_index, good_channel, conv_weight, conv_bias, head_weight, head_bias):
    full_conv, full_bias, full_head = (
        lax.all_gather(conv_weight, "fsdp", axis=1, tiled=True),
        lax.all_gather(conv_bias, "fsdp", axis=1, tiled=True),
        lax.all_gather(head_weight, "fsdp", axis=1, tiled=True),
    )
    grad_kernel, grad_bias, grad_head, grad_hbias, grad_features = local_grads(
        features, pick_index, good_channel, full_conv, full_bias, full_head, head_bias
    )
    owned = lax.psum_scatter(grad_kernel, "dp", scatter_dimension=0, tiled=True)
    owned = lax.psum_scatter(owned, "fsdp", scatter_dimension=1, tiled=True)
    summed = lax.psum((grad_bias, grad_head, grad_hbias), "dp")
    bias_part, head_part = (
        lax.psum_scatter(summed[0], "fsdp", scatter_dimension=1, tiled=True),
        lax.psum_scatter(summed[1], "fsdp", scatter_dimension=1, tiled=True),
    )
    hbias_total = lax.psum(summed[2], "fsdp")
    return (owned, bias_part, head_part, hbias_total, grad_features)


def solution(mesh):
    return jax.shard_map(
        on_device,
        mesh=mesh,
        in_specs=(
            P(("dp", "fsdp"), None, None, None),
            P(("dp", "fsdp"), None, None),
            P(("dp", "fsdp"), None),
            P(None, "fsdp"),
            P(None, "fsdp"),
            P(None, "fsdp"),
            P(),
        ),
        out_specs=(
            P("dp", "fsdp"),
            P(None, "fsdp"),
            P(None, "fsdp"),
            P(),
            P(("dp", "fsdp"), None, None, None),
        ),
        check_vma=False,
    )
```

profile of v0, /device:TPU:0, one launch (start us, length us, event | category | flops | bytes accessed | tf_op | source)
XLA Modules:
  0.0 184.8 jit_solution(14172446390495054646)
XLA Ops:
  7.3 0.7 convert_bitcast_fusion.1
  7.9 0.6 dynamic-slice
  9.2 0.9 dynamic-update-slice
  10.0 8.3 %all-reduce.2 = bf16[128]{0:T(256)(128)(2,1)S(1)} all-reduce(bf16[128]{0:T(256)(128)(2,1)S(1)} %dynamic-update-slice), channel_id=1, replica_groups=mesh['dp'=8,'fsdp'=4] {'fsdp'}, use_global_device_ids=true, to_apply=%add.2 | all-reduce | flops 128 | bytes 512
  18.3 0.7 convert_bitcast_fusion
  19.0 5.2 %all-gather = bf16[4,32,2]{1,2,0:T(2,128)(2,1)S(1)} all-gather(bf16[1,32,2]{1,2,0:T(2,128)(2,1)} %bitcast.139), channel_id=1, replica_groups=mesh['dp'=8,'fsdp'=4] {'fsdp'}, dimensions={0}, use_global_device_ids=true | all-gather | bytes 640 | tf_op jit(solution)/shard_map/all_gather | solution.py:78
  24.5 6.0 %all_gather.10 = bf16[1152,128]{0,1:T(8,128)(2,1)S(1)} all-gather(bf16[1152,32]{0,1:T(8,128)(2,1)S(1)} %copy-done.2), channel_id=1, replica_groups=mesh['dp'=8,'fsdp'=4] {'fsdp'}, dimensions={1}, use_global_device_ids=true | all-gather | bytes 368640 | tf_op jit(solution)/shard_map/all_gather | solution.py:76
  30.5 3.5 %pad_slice_fusion.8 = (bf16[1,8,256,128]{3,2,1,0:T(8,128)(2,1)S(1)}, bf16[1,8,256,128]{3,2,1,0:T(8,128)(2,1)S(1)}, bf16[1,8,256,128]{3,2,1,0:T(8,128)(2,1)S(1)},...) fusion(bf16[1,8,256,128]{3,2,1,0:T(8,128)(2,1)} %param.7), kind=kLoop, calls=%fused_computation.51 | loop fusion | bytes 4718592 | tf_op jit(solution)/shard_map/slice | solution.py:18
  33.9 0.3 convolution_add_fusion.16
  34.2 0.3 convolution_add_fusion.15
  34.5 0.3 convolution_add_fusion.14
  34.9 0.3 convolution_add_fusion.13
  35.2 0.7 copy-done
  35.9 0.3 convolution_add_fusion.12
  36.2 0.3 convolution_add_fusion.11
  36.5 0.3 convolution_add_fusion.10
  36.8 0.3 convolution_add_fusion.9
  37.1 0.5 multiply_convert_fusion
  37.6 0.6 copy-done.3
  38.2 0.4 convert_reduce_fusion.1
  38.6 0.6 convert_reduce_fusion
  39.2 0.3 convolution_dynamic-update-slice_fusion.7
  39.5 0.3 convolution_dynamic-update-slice_fusion.6
  39.9 0.3 convolution_dynamic-update-slice_fusion.5
  40.2 0.3 convolution_dynamic-update-slice_fusion.4
  40.6 0.3 fusion.10
  40.9 0.3 convolution_dynamic-update-slice_fusion.3
  41.2 0.3 convolution_dynamic-update-slice_fusion.2
  41.6 0.3 convolution_dynamic-update-slice_fusion.1
  41.9 0.3 convolution_dynamic-update-slice_fusion
  42.3 0.8 copy-done.1
  43.2 0.7 copy.19
  44.0 1.0 convolution_bitcast_fusion.1
  45.0 0.8 pad_slice_fusion
  46.1 0.3 convolution_add_fusion.7
  46.4 0.3 convolution_add_fusion.6
  46.7 0.3 convolution_add_fusion.5
  47.0 0.3 convolution_add_fusion.4
  47.3 0.3 convolution_add_fusion.3
  48.1 58.1 %reduce-scatter.11.cloned.1.call-done = f32[144,128]{1,0:T(8,128)} async-done(((f32[1152,128]{1,0:T(8,128)}), f32[144,128]{1,0:T(8,128)}) %reduce-scatter.11.cloned.1.call-update) | async-done | bytes 73744 | tf_op jit(solution)/shard_map/reduce_scatter | solution.py:83
  106.2 1.6 copy.17
  107.9 1.1 fusion.1
  108.9 18.3 %reduce-scatter.15.cloned.1.call-done = f32[32,1]{1,0:T(8,128)} async-done(((f32[128,1]{1,0:T(8,128)}), f32[32,1]{1,0:T(8,128)}) %reduce-scatter.15.cloned.1.call-update) | async-done | bytes 144
  127.2 0.8 copy.20
  128.0 21.1 %reduce-scatter.17.cloned.1.call-done = f32[32,2]{1,0:T(8,128)} async-done(((f32[128,2]{1,0:T(8,128)}), f32[32,2]{1,0:T(8,128)}) %reduce-scatter.17.cloned.1.call-update) | async-done | bytes 272
  149.1 0.8 copy.22
  149.9 21.9 %all-reduce.3 = (f32[1,32]{1,0:T(1,128)}, f32[2,32]{1,0:T(2,128)}, f32[2]{0:T(128)S(1)}) all-reduce(f32[1,32]{1,0:T(1,128)S(1)} %copy.20, f32[2,32]{1,0:T(2,128)S(1)} %copy.22, f32[2]{0:T(128)S(1)} %get-tuple-element.43), channel_id=1, replica_groups=mesh['dp'=8,'fsdp'=4] {'dp'}, use_global_device_ids=true, to_apply=%region_3.4 | all-reduce | flops 98 | bytes 784 | tf_op jit(solution)/shard_map/psum | solution.py:85
  171.8 6.4 %psum.31 = f32[2]{0:T(128)} all-reduce(f32[2]{0:T(128)S(1)} %get-tuple-element.22), channel_id=1, replica_groups=mesh['dp'=8,'fsdp'=4] {'fsdp'}, use_global_device_ids=true, to_apply=%region_9.10 | all-reduce | flops 2 | bytes 16 | tf_op jit(solution)/shard_map/psum | solution.py:90
  (29 shorter events, 1.4 us)
Async XLA Ops:
  7.2 0.8 copy-start.4
  7.2 17.3 %copy-start.2 = (bf16[1152,32]{0,1:T(8,128)(2,1)S(1)}, bf16[1152,32]{0,1:T(8,128)(2,1)}, u32[]{:S(2)}) copy-start(bf16[1152,32]{0,1:T(8,128)(2,1)} %param.10) | copy-start | bytes 221188
  7.2 99.0 %reduce-scatter.11.cloned.1.call-start = ((), (), s32[]{:S(2)}) async-start(), calls=%async_computation.4 | async-start | bytes 663552 | tf_op jit(solution)/shard_map/reduce_scatter | solution.py:83
  34.8 1.0 copy-start
  37.6 0.7 copy-start.3
  42.3 0.8 copy-start.1
  43.1 84.1 %reduce-scatter.15.cloned.1.call-start = ((), (), s32[]{:S(2)}) async-start(), calls=%async_computation.6 | async-start | bytes 81920
  43.9 105.2 %reduce-scatter.17.cloned.1.call-start = ((), (), s32[]{:S(2)}) async-start(), calls=%async_computation.7 | async-start | bytes 81920
  45.0 133.3 %reduce-scatter.13.cloned.1.call-start = ((), (), s32[]{:S(2)}) async-start(), calls=%async_computation.5 | async-start | bytes 163840
Sparse Core Ops, SparseCore 0:
  43.2 62.9 reduce-scatter.10
  108.8 18.4 reduce-scatter.14
  129.7 19.3 reduce-scatter.16
  152.1 19.5 reduce-scatter.12
where the time goes:
time: 185 us
  waiting for transfers between devices  97.5 us (53%)
  blocking collectives  47.8 us (26%)
  between operations  14.7 us (8%)
  local copies, waits for them, and re-layouts  12.1 us (7%)
  matrix products  11.1 us (6%)
    reduce_scatter x1, waiting for transfers between devices, on_device(): owned = lax.psum_scatter(grad_kernel, 'dp', scatter_dimension=0, tiled=True)  58.1 us
    unnamed x7, waiting for transfers between devices  39.4 us
    psum x1, blocking collectives, on_device(): summed = lax.psum((grad_bias, grad_head, grad_hbias), 'dp')  21.9 us
    unnamed x1, blocking collectives  8.31 us
    unnamed x24, local copies, waits for them, and re-layouts  7.84 us
    psum x1, blocking collectives, on_device(): hbias_total = lax.psum(summed[2], 'fsdp')  6.4 us
    all_gather x1, blocking collectives, on_device(): lax.all_gather(conv_weight, 'fsdp', axis=1, tiled=True)  6 us
    all_gather x1, blocking collectives, on_device(): lax.all_gather(head_weight, 'fsdp', axis=1, tiled=True)  5.16 us
  transfers between devices with their start and end apart: 4, of which 3 were waited for; matrix products, arithmetic and copies ran while one was open for 5% of the time, Pallas kernels for 0%

commit v1 on v0

--- a/solution.py
+++ b/solution.py
@@ -4,6 +4,19 @@
 from jax.sharding import PartitionSpec as P
 
 SIGMA = 20
+
+
+def ring_gather(x, axis, dim):
+    ways = lax.axis_size(axis)
+    up = [(d, (d + 1) % ways) for d in range(ways)]
+    down = [(d, (d - 1) % ways) for d in range(ways)]
+    earlier, later = ([x], [x])
+    for _ in range(ways // 2):
+        earlier.append(lax.ppermute(earlier[-1], axis, up))
+    for _ in range((ways - 1) // 2):
+        later.append(lax.ppermute(later[-1], axis, down))
+    line = jnp.concatenate([*earlier[::-1], *later[1:]], axis=dim)
+    return jnp.roll(line, (lax.axis_index(axis) - ways // 2) * x.shape[dim], axis=dim)
 
 
 def local_grads(features, pick_index, good_channel, conv_weight, conv_bias, head_weight, head_bias):
@@ -73,7 +86,7 @@
 
 def on_device(features, pick_index, good_channel, conv_weight, conv_bias, head_weight, head_bias):
     full_conv, full_bias, full_head = (
-        lax.all_gather(conv_weight, "fsdp", axis=1, tiled=True),
+        ring_gather(conv_weight, "fsdp", 1),
         lax.all_gather(conv_bias, "fsdp", axis=1, tiled=True),
         lax.all_gather(head_weight, "fsdp", axis=1, tiled=True),
     )

time: 185 us -> 192 us (1.038)
  matrix products: 11.1 us -> 31.8 us
  waiting for transfers between devices: 97.5 us -> 83.2 us
  blocking collectives: 47.8 us -> 40 us
  local copies, waits for them, and re-layouts: 12.1 us -> 18 us
  starting transfers between devices: 0.16 us -> 2.72 us
    dot_general x9, matrix products: 3.32 us -> 18.1 us  [local_grads(): jnp.einsum('nd,cd->nc', window, conv_weight[tap_index * width:(tap_index...]
    reduce_scatter x1, waiting for transfers between devices: 58.1 us -> 46.7 us  [on_device(): owned = lax.psum_scatter(grad_kernel, 'dp', scatter_dimension=0, tiled=True)]
    all_gather x1 -> x0, blocking collectives: 6 us -> none  [on_device(): lax.all_gather(conv_weight, 'fsdp', axis=1, tiled=True)]
    dot_general x9, matrix products: 3.06 us -> 8.73 us  [local_grads(): jnp.einsum('nc,nd->cd', window, dpre, preferred_element_type=jnp.float32)]
    unnamed x24 -> x57, local copies, waits for them, and re-layouts: 7.84 us -> 11.4 us
    unnamed x7, waiting for transfers between devices: 39.4 us -> 36.5 us
    ppermute x0 -> x3, starting transfers between devices: none -> 2.55 us  [the longest x1 1.99 us: ring_gather(): later.append(lax.ppermute(later[-1], axis, down))]
    unnamed x1, blocking collectives: 8.31 us -> 6.3 us
  transfers between devices with their start and end apart: 4 -> 7, of which waited for: 3 -> 3; matrix products, arithmetic and copies ran while one was open for 5% -> 16% of each run, Pallas kernels for 0% -> 0%
where the time goes in v1:
time: 192 us; the launch traced here: 191 us
  waiting for transfers between devices  83.2 us (43%)
  blocking collectives  40 us (21%)
  matrix products  31.8 us (17%)
  local copies, waits for them, and re-layouts  18 us (9%)
  between operations  14.7 us (8%)
  starting transfers between devices  2.72 us (1%)
    reduce_scatter x1, waiting for transfers between devices, on_device(): owned = lax.psum_scatter(grad_kernel, 'dp', scatter_dimension=0, tiled=True)  46.7 us
    unnamed x7, waiting for transfers between devices  36.5 us
    psum x1, blocking collectives, on_device(): summed = lax.psum((grad_bias, grad_head, grad_hbias), 'dp')  21.9 us
    dot_general x9, matrix products, local_grads(): jnp.einsum('nd,cd->nc', window, conv_weight[tap_index * width:(tap_index...  18.1 us
    unnamed x57, local copies, waits for them, and re-layouts  11.4 us
    dot_general x9, matrix products, local_grads(): jnp.einsum('nc,nd->cd', window, dpre, preferred_element_type=jnp.float32)  8.73 us
    psum x1, blocking collectives, on_device(): hbias_total = lax.psum(summed[2], 'fsdp')  6.4 us
    unnamed x1, blocking collectives  6.3 us
  transfers between devices with their start and end apart: 7, of which 3 were waited for; matrix products, arithmetic and copies ran while one was open for 16% of the time, Pallas kernels for 0%

profile of v1, /device:TPU:0, one launch (start us, length us, event | category | flops | bytes accessed | tf_op | source)
XLA Modules:
  0.0 191.2 jit_solution(10389282130890610651)
XLA Ops:
  7.2 0.5 collective-permute-start
  7.7 2.0 %collective-permute-start.2 = (bf16[1152,32]{0,1:T(8,128)(2,1)}, bf16[1152,32]{0,1:T(8,128)(2,1)S(1)}, u32[]{:S(2)}, u32[]{:S(2)}) collective-permute-start(bf16[1152,32]{0,1:T(8,128)(2,1)} %param.10), channel_id=1, source_target_pairs={{0,3},{1,0},{2,1},{3,2},{4,7},{5,4},{6,5},{7,6},{8,11},{9,8},{10,9... | collective-permute-start | bytes 221192 | tf_op jit(solution)/shard_map/ppermute | solution.py:17
  9.7 0.7 convert_bitcast_fusion
  10.5 0.6 copy-done.14
  11.1 4.5 %pad_slice_fusion.14 = (bf16[1,8,256,128]{3,2,1,0:T(8,128)(2,1)}, bf16[1,8,256,128]{3,2,1,0:T(8,128)(2,1)S(1)}, bf16[1,8,256,128]{3,2,1,0:T(8,128)(2,1)S(1)}, bf...) fusion(bf16[1,8,256,128]{3,2,1,0:T(8,128)(2,1)} %param.7), kind=kLoop, calls=%fused_computation.58 | loop fusion | bytes 4718592 | tf_op jit(solution)/shard_map/slice | solution.py:31
  15.7 0.7 copy-done.17
  16.3 0.6 dynamic-slice
  17.6 0.6 copy-done.15
  18.4 6.3 %all-reduce.2 = bf16[128]{0:T(256)(128)(2,1)S(1)} all-reduce(bf16[128]{0:T(256)(128)(2,1)S(1)} %dynamic-update-slice), channel_id=1, replica_groups=mesh['dp'=8,'fsdp'=4] {'fsdp'}, use_global_device_ids=true, to_apply=%add.2 | all-reduce | flops 128 | bytes 512
  24.8 0.6 copy-done.13
  25.5 5.4 %all-gather = bf16[4,32,2]{1,2,0:T(2,128)(2,1)S(1)} all-gather(bf16[1,32,2]{1,2,0:T(2,128)(2,1)S(1)} %bitcast.141), channel_id=1, replica_groups=mesh['dp'=8,'fsdp'=4] {'fsdp'}, dimensions={0}, use_global_device_ids=true | all-gather | bytes 640 | tf_op jit(solution)/shard_map/all_gather | solution.py:91
  31.1 0.9 copy-done.12
  33.3 0.7 copy-done
  35.0 0.7 copy-done.3
  36.0 0.7 copy-done.4
  36.7 0.7 multiply_convert_fusion
  37.5 0.7 copy-done.16
  38.1 0.4 convert_reduce_fusion.1
  38.5 0.6 convert_reduce_fusion
  39.1 1.0 convolution_dynamic-update-slice_fusion.7
  40.1 1.3 fusion.44
  41.3 1.0 convolution_dynamic-update-slice_fusion.6
  42.4 1.0 convolution_dynamic-update-slice_fusion.5
  43.3 1.0 convolution_dynamic-update-slice_fusion.4
  44.3 1.0 fusion.25
  45.3 1.0 convolution_dynamic-update-slice_fusion.3
  46.3 1.0 convolution_dynamic-update-slice_fusion.2
  47.2 1.0 convolution_dynamic-update-slice_fusion.1
  48.2 1.0 convolution_dynamic-update-slice_fusion
  49.2 2.0 %pad_slice_fusion.7 = (bf16[1,8,256,128]{3,2,1,0:T(8,128)(2,1)}, bf16[1,8,256,128]{3,2,1,0:T(8,128)(2,1)}, bf16[1,8,256,128]{3,2,1,0:T(8,128)(2,1)S(1)}, bf16[1,...) fusion(bf16[1,8,256,128]{3,2,1,0:T(8,128)(2,1)S(1)} %bitcast.105), kind=kLoop, calls=%fused_computation.51 | loop fusion | bytes 4718592 | tf_op jit(solution)/shard_map/slice | solution.py:71
  51.3 1.0 fusion.28
  52.3 1.1 fusion.32
  53.4 0.7 copy.23
  54.1 2.1 %fusion.36 = f32[2048,128]{1,0:T(8,128)} fusion(bf16[2048,128]{1,0:T(8,128)(2,1)S(1)} %bitcast.129, bf16[1152,256]{0,1:T(8,128)(2,1)} %copy-done.11, s32[]{:T(128)S(6)} %add.150, s32[]{:T(128)S(6)} %select_n.14), kind=kOutput, calls=%fused_computation.78 | convolution fusion | flops 67108864 | bytes 1605640 | tf_op jit(solution)/shard_map/nd,cd->nc/dot_general | solution.py:77
  56.2 2.1 %fusion.40 = f32[2048,128]{1,0:T(8,128)} fusion(bf16[2048,128]{1,0:T(8,128)(2,1)S(1)} %bitcast.128, bf16[1152,256]{0,1:T(8,128)(2,1)} %copy-done.11, s32[]{:T(128)S(6)} %add.149, s32[]{:T(128)S(6)} %select_n.14), kind=kOutput, calls=%fused_computation.82 | convolution fusion | flops 67108864 | bytes 1605640 | tf_op jit(solution)/shard_map/nd,cd->nc/dot_general | solution.py:77
  58.3 2.0 %fusion.47 = f32[2048,128]{1,0:T(8,128)} fusion(bf16[2048,128]{1,0:T(8,128)(2,1)S(1)} %bitcast.127, bf16[1152,256]{0,1:T(8,128)(2,1)} %copy-done.11, s32[]{:T(128)S(6)} %add.147, s32[]{:T(128)S(6)} %select_n.14), kind=kOutput, calls=%fused_computation.89 | convolution fusion | flops 67108864 | bytes 1605640 | tf_op jit(solution)/shard_map/nd,cd->nc/dot_general | solution.py:77
  60.4 2.1 %fusion.51 = f32[2048,128]{1,0:T(8,128)} fusion(bf16[2048,128]{1,0:T(8,128)(2,1)S(1)} %bitcast.126, bf16[1152,256]{0,1:T(8,128)(2,1)} %copy-done.11, s32[]{:T(128)S(6)} %add.146, s32[]{:T(128)S(6)} %select_n.14), kind=kOutput, calls=%fused_computation.93 | convolution fusion | flops 67108864 | bytes 1605640 | tf_op jit(solution)/shard_map/nd,cd->nc/dot_general | solution.py:77
  62.5 1.0 convolution_bitcast_fusion.2
  63.5 2.4 %fusion.55 = f32[2048,128]{1,0:T(8,128)} fusion(bf16[2048,128]{1,0:T(8,128)(2,1)} %bitcast.125, bf16[1152,256]{0,1:T(8,128)(2,1)} %copy-done.11, s32[]{:T(128)S(6)} %add.145, s32[]{:T(128)S(6)} %select_n.14), kind=kOutput, calls=%fused_computation.97 | convolution fusion | flops 67108864 | bytes 1605640 | tf_op jit(solution)/shard_map/nd,cd->nc/dot_general | solution.py:77
  65.9 46.7 %reduce-scatter.11.cloned.1.call-done = f32[144,128]{1,0:T(8,128)} async-done(((f32[1152,128]{1,0:T(8,128)}), f32[144,128]{1,0:T(8,128)}) %reduce-scatter.11.cloned.1.call-update) | async-done | bytes 73744 | tf_op jit(solution)/shard_map/reduce_scatter | solution.py:96
  112.7 1.6 copy.21
  114.3 4.0 %fusion.15 = bf16[2048,128]{1,0:T(8,128)(2,1)} fusion(f32[2048,128]{1,0:T(8,128)S(1)} %fusion.28, f32[2048,128]{1,0:T(8,128)S(1)} %fusion.32, f32[2048,128]{1,0:T(8,128)} %fusion.36, f32[2048,128]{1,0:T(8,128)} %fusion.40, f32[2048,128]{1,0:T(8,128)S(1)} %copy-done.5, f32[2048,128]{1,0:T(8,128)} %fusion.47, f32[2048,128]{1,0:T(8,128)} %fusion.51, ...), kind=kOutput, calls=%fused_computation.19 | convolution fusion | flops 69468160 | bytes 9469956 | tf_op jit(solution)/shard_map/nd,cd->nc/dot_general | solution.py:77
  118.3 15.3 %reduce-scatter.15.cloned.1.call-done = f32[32,1]{1,0:T(8,128)} async-done(((f32[128,1]{1,0:T(8,128)}), f32[32,1]{1,0:T(8,128)}) %reduce-scatter.15.cloned.1.call-update) | async-done | bytes 144
  133.7 0.8 copy.24
  134.5 21.1 %reduce-scatter.17.cloned.1.call-done = f32[32,2]{1,0:T(8,128)} async-done(((f32[128,2]{1,0:T(8,128)}), f32[32,2]{1,0:T(8,128)}) %reduce-scatter.17.cloned.1.call-update) | async-done | bytes 272
  155.6 0.8 copy.26
  156.4 21.9 %all-reduce.3 = (f32[1,32]{1,0:T(1,128)}, f32[2,32]{1,0:T(2,128)}, f32[2]{0:T(128)S(1)}) all-reduce(f32[1,32]{1,0:T(1,128)S(1)} %copy.24, f32[2,32]{1,0:T(2,128)S(1)} %copy.26, f32[2]{0:T(128)S(1)} %get-tuple-element.43), channel_id=1, replica_groups=mesh['dp'=8,'fsdp'=4] {'dp'}, use_global_device_ids=true, to_apply=%region_3.4 | all-reduce | flops 98 | bytes 784 | tf_op jit(solution)/shard_map/psum | solution.py:98
  178.3 6.4 %psum.31 = f32[2]{0:T(128)} all-reduce(f32[2]{0:T(128)S(1)} %get-tuple-element.22), channel_id=1, replica_groups=mesh['dp'=8,'fsdp'=4] {'fsdp'}, use_global_device_ids=true, to_apply=%region_9.10 | all-reduce | flops 2 | bytes 16 | tf_op jit(solution)/shard_map/psum | solution.py:103
  (68 shorter events, 3.4 us)
Async XLA Ops:
  7.2 105.5 %reduce-scatter.11.cloned.1.call-start = ((), (), s32[]{:S(2)}) async-start(), calls=%async_computation.4 | async-start | bytes 663552 | tf_op jit(solution)/shard_map/reduce_scatter | solution.py:96
  7.2 17.5 %collective-permute-start = (bf16[1152,32]{0,1:T(8,128)(2,1)}, bf16[1152,32]{0,1:T(8,128)(2,1)S(1)}, u32[]{:S(2)}, u32[]{:S(2)}) collective-permute-start(bf16[1152,32]{0,1:T(8,128)(2,1)} %param.10), channel_id=1, source_target_pairs={{0,1},{1,2},{2,3},{3,0},{4,5},{5,6},{6,7},{7,4},{8,9},{9,10},{10,1... | collective-permute-start | bytes 221192 | tf_op jit(solution)/shard_map/ppermute | solution.py:15
  7.7 24.2 %collective-permute-start.2 = (bf16[1152,32]{0,1:T(8,128)(2,1)}, bf16[1152,32]{0,1:T(8,128)(2,1)S(1)}, u32[]{:S(2)}, u32[]{:S(2)}) collective-permute-start(bf16[1152,32]{0,1:T(8,128)(2,1)} %param.10), channel_id=1, source_target_pairs={{0,3},{1,0},{2,1},{3,2},{4,7},{5,4},{6,5},{7,6},{8,11},{9,8},{10,9... | collective-permute-start | bytes 221192 | tf_op jit(solution)/shard_map/ppermute | solution.py:17
  10.4 0.7 copy-start.14
  15.6 19.0 %copy-start.1 = (bf16[1,8,256,128]{3,2,1,0:T(8,128)(2,1)}, bf16[1,8,256,128]{3,2,1,0:T(8,128)(2,1)S(1)}, u32[]{:S(2)}) copy-start(bf16[1,8,256,128]{3,2,1,0:T(8,128)(2,1)S(1)} %get-tuple-element.32) | copy-start | bytes 1572868
  15.7 0.7 copy-start.17
  17.5 0.7 copy-start.15
  24.7 6.3 %collective-permute-start.1 = (bf16[1152,32]{0,1:T(8,128)(2,1)S(1)}, bf16[1152,32]{0,1:T(8,128)(2,1)S(1)}, u32[]{:S(2)}, u32[]{:S(2)}) collective-permute-start(bf16[1152,32]{0,1:T(8,128)(2,1)S(1)} %collective-permute-done), channel_id=1, source_target_pairs={{0,1},{1,2},{2,3},{3,0},{4,5},{5,6},{6,7},{7,4},{8,9},{9,10},{10,1... | collective-permute-start | bytes 221192 | tf_op jit(solution)/shard_map/ppermute | solution.py:15
  24.8 0.7 copy-start.13
  31.0 0.9 copy-start.12
  32.0 8.1 %copy-start.11 = (bf16[1152,256]{0,1:T(8,128)(2,1)}, bf16[1152,256]{0,1:T(8,128)(2,1)S(1)}, u32[]{:S(2)}) copy-start(bf16[1152,256]{0,1:T(8,128)(2,1)S(1)} %constant_dynamic-update-slice_fusion) | copy-start | bytes 1769476
  33.0 1.0 copy-start
  34.6 1.0 copy-start.3
  35.7 1.0 copy-start.4
  37.4 1.7 copy-start.9
  37.4 0.7 copy-start.16
  41.3 1.0 copy-start.2
  49.2 84.5 %reduce-scatter.15.cloned.1.call-start = ((), (), s32[]{:S(2)}) async-start(), calls=%async_computation.6 | async-start | bytes 81920
  52.3 1.8 copy-start.8
  54.1 2.1 %copy-start.7 = (bf16[1,8,256,128]{3,2,1,0:T(8,128)(2,1)S(1)}, bf16[1,8,256,128]{3,2,1,0:T(8,128)(2,1)}, u32[]{:S(2)}) copy-start(bf16[1,8,256,128]{3,2,1,0:T(8,128)(2,1)} %get-tuple-element.27) | copy-start | bytes 1572868
  56.2 2.1 %copy-start.6 = (bf16[1,8,256,128]{3,2,1,0:T(8,128)(2,1)S(1)}, bf16[1,8,256,128]{3,2,1,0:T(8,128)(2,1)}, u32[]{:S(2)}) copy-start(bf16[1,8,256,128]{3,2,1,0:T(8,128)(2,1)} %get-tuple-element.26) | copy-start | bytes 1572868
  60.4 2.1 %copy-start.10 = (bf16[2048,128]{1,0:T(8,128)(2,1)S(1)}, bf16[2048,128]{1,0:T(8,128)(2,1)}, u32[]{:S(2)}) copy-start(bf16[2048,128]{1,0:T(8,128)(2,1)} %copy-done.9) | copy-start | bytes 1572868
  62.4 93.1 %reduce-scatter.17.cloned.1.call-start = ((), (), s32[]{:S(2)}) async-start(), calls=%async_computation.7 | async-start | bytes 81920
  63.5 50.9 %copy-start.5 = (f32[2048,128]{1,0:T(8,128)S(1)}, f32[2048,128]{1,0:T(8,128)}, u32[]{:S(2)}) copy-start(f32[2048,128]{1,0:T(8,128)} %fusion.44) | copy-start | bytes 3145732
  63.5 121.2 %reduce-scatter.13.cloned.1.call-start = ((), (), s32[]{:S(2)}) async-start(), calls=%async_computation.5 | async-start | bytes 163840
Sparse Core Ops, SparseCore 0:
  49.3 63.2 reduce-scatter.10
  115.2 18.4 reduce-scatter.14
  136.1 19.4 reduce-scatter.16
  158.6 19.5 reduce-scatter.12
